TPU v7x, 256 devices: a whole 4x4x8 slice. The times are simulated.
256 devices in a mesh: prow: 16 (over x, y), pcol: 16 (over z, core).
Axes of the slice: x: 4, y: 4, z: 8, core: 2. Of those that a mesh axis runs over, the one named last changes fastest.
Arguments:
- inverse_tiles: float32 [24576, 24576], P('prow', 'pcol'), may hold values from -6 to 6
- factor_rows: float32 [24576, 512], P('prow'), may hold values from -0.0390625 to 0.0390625
- diag_inverse: float32 [512, 512], P('prow', 'pcol'), may hold values from -6 to 6
- pattern: int32 [192], replicated, may hold values from 0 to 1, as said below
Outputs:
- column_block: float32 [24576, 512], P(('prow', 'pcol'))
- diagonal_block: float32 [512, 512], P('prow', 'pcol')
Inputs may be any that keep to these rules, and one draw needn't show every extreme that they name: `pattern`: 1 where the block of ancestor rows lies in the supernode's structure, else 0; the first block always lies in it and the last never.
All inputs are finite; a program needn't handle non-finite values.
Results may differ from a plain program's by a relative error of at most 0.000078.
Values sent between devices are 32-bit elements; how exact they have to be, the bound alone decides.
A program may use at most 64 MiB of HBM per device.

v0:
```python
import jax
import jax.numpy as jnp
from jax import lax
from jax.sharding import PartitionSpec as P

BLK = 128


def broadcast(shard, axis, root):
    mine = lax.axis_index(axis) == root
    return lax.psum(jnp.where(mine, shard, jnp.zeros_like(shard)), axis)


def row_select(pattern, first_row, row_count):
    global_rows = first_row + lax.iota(jnp.int32, row_count)
    block_ids = global_rows // BLK
    blocks = lax.iota(jnp.int32, pattern.shape[0])
    match = block_ids[:, None] == blocks[None, :]
    return jnp.sum(jnp.where(match, pattern[None, :], 0), axis=1).astype(jnp.float32)


def local(inverse_tiles, factor_rows, diag_inverse, pattern):
    n_row = lax.axis_size("prow")
    n_col = lax.axis_size("pcol")
    row_index = lax.axis_index("prow")
    col_index = lax.axis_index("pcol")
    tile_rows = inverse_tiles.shape[0]
    width = factor_rows.shape[1]
    col_ratio = n_col // n_row
    tile_mask = row_select(pattern, row_index * tile_rows, tile_rows)
    masked_rows = factor_rows * tile_mask[:, None]
    root_index = col_index // col_ratio
    column_factor = broadcast(masked_rows, "prow", root_index)
    out_rows = tile_rows // n_col
    own_mask = lax.dynamic_slice_in_dim(tile_mask, col_index * out_rows, out_rows, 0)
    summed = lax.psum_scatter(
        jnp.dot(
            inverse_tiles,
            column_factor,
            precision=lax.Precision.HIGHEST,
            preferred_element_type=jnp.float32,
        ),
        "pcol",
        scatter_dimension=0,
        tiled=True,
    )
    column_block = -summed * own_mask[:, None]
    own_factor = lax.dynamic_slice_in_dim(masked_rows, col_index * out_rows, out_rows, 0)
    correction = jnp.dot(
        own_factor.T,
        column_block,
        precision=lax.Precision.HIGHEST,
        preferred_element_type=jnp.float32,
    )
    share_rows = width // n_row
    share_cols = width // n_col
    total = lax.psum(correction, ("prow", "pcol"))
    mine = lax.dynamic_slice_in_dim(total, row_index * share_rows, share_rows, 0)
    mine = lax.dynamic_slice_in_dim(mine, col_index * share_cols, share_cols, 1)
    diagonal_block = diag_inverse - mine
    return (column_block, diagonal_block)


def solution(mesh):
    return jax.shard_map(
        local,
        mesh=mesh,
        in_specs=(P("prow", "pcol"), P("prow", None), P("prow", "pcol"), P()),
        out_specs=(P(("prow", "pcol"), None), P("prow", "pcol")),
        check_vma=False,
    )
```

profile of v0, /device:TPU:2, one launch (start us, length us, event | category | flops | bytes accessed | tf_op | source)
XLA Modules:
  0.0 486.7 jit_solution(2618782349382456584)
XLA Ops:
  7.2 0.0 all-reduce.3.cloned.1.call-start
  7.2 0.9 select_reduce_fusion
  8.2 4.1 broadcast_select_fusion
  12.2 0.0 all-reduce.3.cloned.1.call-update
  12.3 0.0 reduce-scatter.4.cloned.1.call-start
  12.3 108.1 %all-reduce.3.cloned.1.call-done = f32[1536,512]{1,0:T(8,128)} async-done(((f32[1536,512]{1,0:T(8,128)}), f32[1536,512]{1,0:T(8,128)}) %all-reduce.3.cloned.1.call-update) | async-done | bytes 3145744 | tf_op jit(solution)/shard_map/psum | solution.py:11
  120.4 33.8 %convolution_bitcast_fusion = f32[1536,512]{0,1:T(8,128)} fusion(f32[1536,512]{1,0:T(8,128)} %all-reduce.3.cloned.1.call-done, f32[1536,1536]{1,0:T(8,128)} %param.4), kind=kOutput, calls=%fused_computation | convolution fusion | flops 14495514624 | bytes 15728640 | tf_op jit(solution)/shard_map/dot_general | solution.py:37
  154.1 3.5 copy.9
  157.7 0.0 copy-start
  157.7 0.0 reduce-scatter.4.cloned.1.call-update
  157.7 0.0 all-reduce.5.cloned.1.call-start
  157.8 0.1 dynamic_slice.10
  157.9 61.0 %reduce-scatter.4.cloned.1.call-done = f32[96,512]{1,0:T(8,128)} async-done(((f32[1536,512]{1,0:T(8,128)}), f32[96,512]{1,0:T(8,128)}) %reduce-scatter.4.cloned.1.call-update) | async-done | bytes 196624
  218.8 1.8 copy.10
  220.6 1.0 negate_multiply_fusion
  221.6 2.1 fusion
  223.6 0.0 all-reduce.5.cloned.1.call-update
  223.7 0.8 copy.8
  224.5 254.3 %all-reduce.5.cloned.1.call-done = f32[512,512]{1,0:T(8,128)} async-done(((f32[512,512]{1,0:T(8,128)}), f32[512,512]{1,0:T(8,128)}) %all-reduce.5.cloned.1.call-update) | async-done | bytes 1048592 | tf_op jit(solution)/shard_map/psum | solution.py:57
  478.8 0.0 copy-done
  478.8 1.5 dynamic-slice_subtract_fusion
  (2 shorter events, 0.0 us)
Async XLA Ops:
  7.2 113.2 %all-reduce.3.cloned.1.call-start = ((), (), s32[]{:S(2)}) async-start(), calls=%async_computation.1 | async-start | bytes 6291456 | tf_op jit(solution)/shard_map/psum | solution.py:11
  12.3 206.6 %reduce-scatter.4.cloned.1.call-start = ((), (), s32[]{:S(2)}) async-start(), calls=%async_computation.3 | async-start | bytes 3342336
  157.7 321.1 %copy-start = (f32[32,32]{1,0:T(8,128)S(1)}, f32[32,32]{1,0:T(8,128)}, u32[]{:S(2)}) copy-start(f32[32,32]{1,0:T(8,128)} %param.6) | copy-start | bytes 12292
  157.7 321.0 %all-reduce.5.cloned.1.call-start = ((), (), s32[]{:S(2)}) async-start(), calls=%async_computation.2 | async-start | bytes 2097152 | tf_op jit(solution)/shard_map/psum | solution.py:57
Sparse Core Ops, SparseCore 0:
  12.4 107.9 all-reduce.2
  157.8 60.9 reduce-scatter.3
  224.3 254.4 all-reduce.4
where the time goes:
time: 487 us
  waiting for transfers between devices  423 us (87%)
  matrix products  35.8 us (7%)
  between operations  13.8 us (3%)
  other arithmetic  7.43 us (2%)
  local copies, waits for them, and re-layouts  6.18 us (1%)
    psum x1, waiting for transfers between devices, local(): total = lax.psum(correction, ('prow', 'pcol'))  254 us
    psum x1, waiting for transfers between devices, broadcast(): return lax.psum(jnp.where(mine, shard, jnp.zeros_like(shard)), axis)  108 us
    unnamed x4, waiting for transfers between devices  61 us
    dot_general x1, matrix products, local(): jnp.dot(inverse_tiles, column_factor, precision=lax.Precision.HIGHEST, pr...  33.8 us
  transfers between devices with their start and end apart: 3, of which 3 were waited for; matrix products, arithmetic and copies ran while one was open for 0% of the time, Pallas kernels for 0%

commit v1 on v0

--- a/solution.py
+++ b/solution.py
@@ -54,7 +54,7 @@
     )
     share_rows = width // n_row
     share_cols = width // n_col
-    total = lax.psum(correction, ("prow", "pcol"))
+    total = lax.psum(lax.psum(correction, "prow"), "pcol")
     mine = lax.dynamic_slice_in_dim(total, row_index * share_rows, share_rows, 0)
     mine = lax.dynamic_slice_in_dim(mine, col_index * share_cols, share_cols, 1)
     diagonal_block = diag_inverse - mine

time: 487 us -> 441 us (0.906)
  waiting for transfers between devices: 423 us -> 377 us
    psum x1 -> x2, waiting for transfers between devices: 254 us -> 208 us  [local(): total = lax.psum(lax.psum(correction, 'prow'), 'pcol')]
    unnamed x4 -> x5, waiting for transfers between devices: 61 us -> 61 us
  transfers between devices with their start and end apart: 3 -> 4, of which waited for: 3 -> 4; matrix products, arithmetic and copies ran while one was open for 0% -> 0% of each run, Pallas kernels for 0% -> 0%
where the time goes in v1:
time: 441 us; the launch traced here: 440 us
  waiting for transfers between devices  377 us (85%)
  matrix products  35.8 us (8%)
  between operations  13.8 us (3%)
  other arithmetic  7.43 us (2%)
  local copies, waits for them, and re-layouts  6.19 us (1%)
    psum x2, waiting for transfers between devices, local(): total = lax.psum(lax.psum(correction, 'prow'), 'pcol')  208 us
    psum x1, waiting for transfers between devices, broadcast(): return lax.psum(jnp.where(mine, shard, jnp.zeros_like(shard)), axis)  108 us
    unnamed x5, waiting for transfers between devices  61 us
    dot_general x1, matrix products, local(): jnp.dot(inverse_tiles, column_factor, precision=lax.Precision.HIGHEST, pr...  33.8 us
  transfers between devices with their start and end apart: 4, of which 4 were waited for; matrix products, arithmetic and copies ran while one was open for 0% of the time, Pallas kernels for 0%

profile of v1, /device:TPU:2, one launch (start us, length us, event | category | flops | bytes accessed | tf_op | source)
XLA Modules:
  0.0 440.4 jit_solution(15949288918015220223)
XLA Ops:
  7.2 0.0 all-reduce.4.cloned.1.call-start
  7.2 0.9 select_reduce_fusion
  8.2 4.1 broadcast_select_fusion
  12.2 0.0 all-reduce.4.cloned.1.call-update
  12.3 0.0 reduce-scatter.4.cloned.1.call-start
  12.3 108.1 %all-reduce.4.cloned.1.call-done = f32[1536,512]{1,0:T(8,128)} async-done(((f32[1536,512]{1,0:T(8,128)}), f32[1536,512]{1,0:T(8,128)}) %all-reduce.4.cloned.1.call-update) | async-done | bytes 3145744 | tf_op jit(solution)/shard_map/psum | solution.py:11
  120.4 33.8 %convolution_bitcast_fusion = f32[1536,512]{0,1:T(8,128)} fusion(f32[1536,512]{1,0:T(8,128)} %all-reduce.4.cloned.1.call-done, f32[1536,1536]{1,0:T(8,128)} %param.4), kind=kOutput, calls=%fused_computation | convolution fusion | flops 14495514624 | bytes 15728640 | tf_op jit(solution)/shard_map/dot_general | solution.py:37
  154.1 3.5 copy.9
  157.7 0.0 reduce-scatter.4.cloned.1.call-update
  157.7 0.0 copy-start
  157.7 0.0 all-reduce.6.cloned.1.call-start
  157.8 0.1 dynamic_slice.10
  157.9 61.0 %reduce-scatter.4.cloned.1.call-done = f32[96,512]{1,0:T(8,128)} async-done(((f32[1536,512]{1,0:T(8,128)}), f32[96,512]{1,0:T(8,128)}) %reduce-scatter.4.cloned.1.call-update) | async-done | bytes 196624
  218.8 1.8 copy.10
  220.6 1.0 negate_multiply_fusion
  221.6 2.1 fusion
  223.6 0.0 all-reduce.6.cloned.1.call-update
  223.7 0.0 all-reduce.8.cloned.1.call-start
  223.7 95.4 %all-reduce.6.cloned.1.call-done = f32[512,512]{1,0:T(8,128)} async-done(((f32[512,512]{1,0:T(8,128)}), f32[512,512]{1,0:T(8,128)}) %all-reduce.6.cloned.1.call-update) | async-done | bytes 1048592 | tf_op jit(solution)/shard_map/psum | solution.py:57
  319.1 0.0 all-reduce.8.cloned.1.call-update
  319.1 0.8 copy.8
  319.9 112.5 %all-reduce.8.cloned.1.call-done = f32[512,512]{1,0:T(8,128)} async-done(((f32[512,512]{1,0:T(8,128)}), f32[512,512]{1,0:T(8,128)}) %all-reduce.8.cloned.1.call-update) | async-done | bytes 1048592 | tf_op jit(solution)/shard_map/psum | solution.py:57
  432.4 0.0 copy-done
  432.4 1.5 dynamic-slice_subtract_fusion
  (2 shorter events, 0.0 us)
Async XLA Ops:
  7.2 113.2 %all-reduce.4.cloned.1.call-start = ((), (), s32[]{:S(2)}) async-start(), calls=%async_computation.1 | async-start | bytes 6291456 | tf_op jit(solution)/shard_map/psum | solution.py:11
  12.3 206.6 %reduce-scatter.4.cloned.1.call-start = ((), (), s32[]{:S(2)}) async-start(), calls=%async_computation.4 | async-start | bytes 3342336
  157.7 274.6 %copy-start = (f32[32,32]{1,0:T(8,128)S(1)}, f32[32,32]{1,0:T(8,128)}, u32[]{:S(2)}) copy-start(f32[32,32]{1,0:T(8,128)} %param.6) | copy-start | bytes 12292
  157.7 161.3 %all-reduce.6.cloned.1.call-start = ((), (), s32[]{:S(2)}) async-start(), calls=%async_computation.2 | async-start | bytes 2097152 | tf_op jit(solution)/shard_map/psum | solution.py:57
  223.7 208.7 %all-reduce.8.cloned.1.call-start = ((), (), s32[]{:S(2)}) async-start(), calls=%async_computation.3 | async-start | bytes 2097152 | tf_op jit(solution)/shard_map/psum | solution.py:57
Sparse Core Ops, SparseCore 0:
  12.4 107.9 all-reduce.3
  157.8 60.9 reduce-scatter.3
  223.8 95.2 all-reduce.5
  321.2 111.0 all-reduce.7
